TPU v7x, 32 devices: a whole 2x2x4 slice. The times are simulated.
32 devices in a mesh: groups: 2 (over x), heads: 8 (over z, y), query: 2 (over core).
Axes of the slice: x: 2, y: 2, z: 4, core: 2. Of those that a mesh axis runs over, the one named last changes fastest.
Arguments:
- q_compressed: bfloat16 [256, 1536], P(('groups', 'heads', 'query')), parts along dimension 0, may hold values from -6 to 6
- new_latent: bfloat16 [256, 576], P(('groups', 'heads', 'query')), parts along dimension 0, may hold values from -6 to 6
- cached_latent: bfloat16 [2048, 576], P(('groups', 'heads', 'query')), parts along dimension 0
- latent_gain: float32 [512], replicated, may hold values from 0.1 to 1.9
- cached_length: int32 [2], P('groups'), parts along dimension 0, may hold values from 1 to 1024, as said below
- w_q_nope: bfloat16 [1536, 4096], P(None, 'heads'), may hold values from -0.15625 to 0.15625
- w_q_rope: bfloat16 [1536, 2048], P(None, 'heads'), may hold values from -0.15625 to 0.15625
- w_uk: bfloat16 [512, 4096], P(None, 'heads'), may hold values from -0.25 to 0.25
- w_uv: bfloat16 [512, 4096], P(None, 'heads'), may hold values from -0.25 to 0.25
- w_out: bfloat16 [4096, 7168], P('heads'), may hold values from -0.75 to 0.75
Outputs:
- attended: bfloat16 [256, 7168], P(('groups', 'heads', 'query')), parts along dimension 0
There are 2 independent parts, one for each index of `groups`. A program takes and returns all parts, laid end to end along the dimension named above; an argument that names none is the same for every part. Nothing has to cross between parts.
Inputs may be any that keep to these rules, and one draw needn't show every extreme that they name: `cached_length`: live cache slots; the span follows them.
All inputs are finite; a program needn't handle non-finite values.
Results may differ from a plain program's by a relative error of at most 0.014.
The roundings to bfloat16 on the way count: a program that leaves them out, or rounds other values in their place, can miss the bound.
Values may be sent and summed in bfloat16 or wider, within the bound.
A program may use at most 128 MiB of HBM per device.

v0:
```python
import jax
import jax.numpy as jnp
from jax import lax
from jax.sharding import PartitionSpec as P

KR = 512
RD = 64
ND = 128
VD = 128
HEADS_DEV = 4


def rotate(vectors, positions):
    half = vectors.shape[-1] // 2
    freq = 10000.0 ** (-2.0 * jnp.arange(half, dtype=jnp.float32) / vectors.shape[-1])
    angle = positions.astype(jnp.float32)[:, None] * freq[None, :]
    while angle.ndim < vectors.ndim:
        angle = angle[:, None, :]
    first = vectors[..., :half]
    second = vectors[..., half:]
    return jnp.concatenate(
        [
            first * jnp.cos(angle) - second * jnp.sin(angle),
            second * jnp.cos(angle) + first * jnp.sin(angle),
        ],
        axis=-1,
    )


def normalize_new(raw, gain, positions):
    latent = raw[:, :KR].astype(jnp.float32)
    latent = latent * lax.rsqrt(jnp.mean(latent * latent, axis=-1, keepdims=True) + 1e-06) * gain
    turned = rotate(raw[:, KR:].astype(jnp.float32), positions)
    return jnp.concatenate([latent, turned], axis=-1).astype(jnp.bfloat16)


def collect(cached_part, new_part):
    return (
        lax.all_gather(cached_part, ("heads", "query"), axis=0, tiled=True),
        lax.all_gather(new_part, ("heads", "query"), axis=0, tiled=True),
    )


def shards(
    q_compressed,
    new_latent,
    cached_latent,
    latent_gain,
    cached_length,
    w_q_nope,
    w_q_rope,
    w_uk,
    w_uv,
    w_out,
):
    n_query = lax.axis_size("query")
    query_index = lax.axis_index("query")
    heads_index = lax.axis_index("heads")
    tok_dev = q_compressed.shape[0]
    ctx_len = cached_length[0]
    own_tokens = (heads_index * n_query + query_index) * tok_dev + jnp.arange(
        tok_dev, dtype=jnp.int32
    )
    fresh_own = normalize_new(new_latent, latent_gain, ctx_len + own_tokens)
    cache_all, fresh_all = collect(cached_latent, fresh_own)
    span = fresh_all.shape[0]
    keys = jnp.concatenate([cache_all, fresh_all], axis=0)
    ctx = cache_all.shape[0]
    latents = keys[:, :KR]
    q_rows = lax.all_gather(q_compressed, "heads", axis=0, tiled=True)
    rows = q_rows.shape[0]
    local = jnp.arange(rows, dtype=jnp.int32)
    row_tokens = (local // tok_dev * n_query + query_index) * tok_dev + local % tok_dev
    q_nope = jnp.dot(q_rows, w_q_nope, preferred_element_type=jnp.float32).astype(jnp.bfloat16)
    q_rope = jnp.dot(q_rows, w_q_rope, preferred_element_type=jnp.float32).reshape(
        rows, HEADS_DEV, RD
    )
    q_rope = rotate(q_rope, ctx_len + row_tokens).astype(jnp.bfloat16)
    q_lat = jnp.einsum(
        "thd,khd->htk",
        q_nope.reshape(rows, HEADS_DEV, ND),
        w_uk.reshape(KR, HEADS_DEV, ND),
        preferred_element_type=jnp.float32,
    ).astype(jnp.bfloat16)
    q_all = jnp.concatenate([q_lat, jnp.transpose(q_rope, (1, 0, 2))], axis=-1)
    scores = jnp.einsum("htc,kc->htk", q_all, keys, preferred_element_type=jnp.float32) * (
        ND + RD
    ) ** (-0.5)
    kidx = jnp.arange(ctx + span, dtype=jnp.int32)[None, :]
    live = jnp.where(kidx < ctx, kidx < ctx_len, kidx - ctx <= row_tokens[:, None])
    scores = jnp.where(live[None, :, :], scores, -1e30)
    top = jnp.max(scores, axis=-1, keepdims=True)
    expo = jnp.exp(scores - top)
    weights = (expo / jnp.sum(expo, axis=-1, keepdims=True)).astype(jnp.bfloat16)
    o_lat = jnp.einsum("htk,kc->htc", weights, latents, preferred_element_type=jnp.float32).astype(
        jnp.bfloat16
    )
    values = jnp.einsum(
        "htc,che->the", o_lat, w_uv.reshape(KR, HEADS_DEV, VD), preferred_element_type=jnp.float32
    ).astype(jnp.bfloat16)
    values = values.reshape(rows, HEADS_DEV * VD)
    return lax.psum_scatter(
        jnp.dot(values, w_out, preferred_element_type=jnp.float32).astype(jnp.bfloat16),
        "heads",
        scatter_dimension=0,
        tiled=True,
    )


def solution(mesh):
    placed = (
        P(("groups", "heads", "query"), None),
        P(("groups", "heads", "query"), None),
        P(("groups", "heads", "query"), None),
        P(),
        P("groups"),
        P(None, "heads"),
        P(None, "heads"),
        P(None, "heads"),
        P(None, "heads"),
        P("heads", None),
    )
    return jax.shard_map(
        shards,
        mesh=mesh,
        in_specs=placed,
        out_specs=P(("groups", "heads", "query"), None),
        check_vma=False,
    )
```

profile of v0, /device:TPU:0, one launch (start us, length us, event | category | flops | bytes accessed | tf_op | source)
XLA Modules:
  0.0 146.9 jit_solution(11189148536559300682)
XLA Ops:
  6.5 0.0 copy-start
  6.5 0.0 all-gather.2.cloned.1.call-start
  6.5 0.7 all-gather.2.cloned.1.call-update
  7.3 0.0 reduce-scatter.2.cloned.1.call-start
  7.3 0.8 fusion.37
  8.1 0.7 slice_convert_fusion
  9.5 32.8 %all_gather.9 = bf16[64,1536]{1,0:T(8,128)(2,1)S(1)} all-gather(bf16[8,1536]{1,0:T(8,128)(2,1)} %param.10), channel_id=1, replica_groups=mesh['groups'=2,'heads'=8,'query'=2] {'heads'}, dimensions={0}, use_global_device_ids=true | all-gather | bytes 221184 | tf_op jit(solution)/shard_map/all_gather | solution.py:70
  42.3 0.8 fusion.39
  43.1 1.4 fusion.70
  44.4 0.1 fusion.45
  44.6 0.1 pad_maximum_fusion.1
  44.6 21.8 %all_gather.11 = bf16[128,576]{1,0:T(8,128)(2,1)S(1)} all-gather(bf16[8,576]{1,0:T(8,128)(2,1)S(1)} %pad_maximum_fusion.1), channel_id=1, replica_groups=mesh['groups'=2,'heads'=8,'query'=2] {'heads','query'}, dimensions={0}, use_global_device_ids=true | all-gather | bytes 156672 | tf_op jit(solution)/shard_map/all_gather | solution.py:40
  66.4 0.1 copy.42
  66.6 0.1 reshape.187
  66.8 0.2 multiply_cosine_fusion
  67.0 0.1 fusion.64
  67.1 0.0 copy-start.1
  67.2 0.1 maximum_bitcast_fusion
  67.3 0.0 copy-done
  67.3 0.4 fusion.16
  67.7 0.5 copy-done.1
  68.2 0.3 convolution_convert_fusion.2
  68.5 0.1 compare_select_fusion
  68.6 0.0 all-gather.2.cloned.1.call-done
  68.6 1.6 %copy.41 = bf16[1024,576]{0,1:T(8,128)(2,1)S(1)} copy(bf16[1024,576]{1,0:T(8,128)(2,1)} %all-gather.2.cloned.1.call-done) | data formatting | bytes 2359296 | tf_op jit(solution)/shard_map/all_gather | solution.py:39
  70.2 1.9 %fusion.65 = (f32[4,64]{1,0:T(4,128)S(1)}, f32[4,64,1152]{2,1,0:T(8,128)}) fusion(bf16[128,576]{0,1:T(8,128)(2,1)S(1)} %copy.42, bf16[1024,576]{0,1:T(8,128)(2,1)S(1)} %copy.41, pred[64,1152]{1,0:T(8,128)(4,1)S(1)} %compare_select_fusion, bf16[4,64,64]{2,1,0:T(8,128)(2,1)S(1)} %maximum_bitcast_fusion, bf16[4,64,512]{2,1,0:T(8,128)(2,1)S(1)} %convolution_convert_fusion.2), kind=kOutput, calls=%fused_computation.79 | convolution fusion | flops 344163456 | bytes 2876416 | tf_op jit(solution)/shard_map/sub | solution.py:93
  72.1 2.1 %fusion.17 = bf16[4,8,8,128]{3,2,1,0:T(8,128)(2,1)S(1)} fusion(bf16[1024,576]{0,1:T(8,128)(2,1)S(1)} %copy.41, bf16[128,576]{0,1:T(8,128)(2,1)S(1)} %copy.42, f32[4,64,1152]{2,1,0:T(8,128)} %get-tuple-element.14, f32[4,64]{1,0:T(4,128)S(1)} %get-tuple-element.13, bf16[512,512]{1,0:T(8,128)(2,1)} %param.18), kind=kOutput, calls=%fused_computation.20 | convolution fusion | flops 338657280 | bytes 3097600 | tf_op jit(solution)/shard_map/htc,che->the/dot_general | solution.py:98
  74.2 5.4 %convolution_convert_fusion = bf16[64,7168]{1,0:T(8,128)(2,1)} fusion(bf16[512,7168]{1,0:T(8,128)(2,1)} %param.19, bf16[4,8,8,128]{3,2,1,0:T(8,128)(2,1)S(1)} %fusion.17), kind=kOutput, calls=%fused_computation.1 | convolution fusion | flops 470220800 | bytes 8323072 | tf_op jit(solution)/shard_map/dot_general | solution.py:103
  79.6 0.0 reduce-scatter.2.cloned.1.call-update
  79.7 60.4 %reduce-scatter.2.cloned.1.call-done = bf16[8,7168]{1,0:T(8,128)(2,1)} async-done(((bf16[64,7168]{1,0:T(8,128)(2,1)}), bf16[8,7168]{1,0:T(8,128)(2,1)}) %reduce-scatter.2.cloned.1.call-update) | async-done | bytes 114704 | tf_op jit(solution)/shard_map/reduce_scatter | solution.py:102
  (8 shorter events, 0.1 us)
Async XLA Ops:
  6.5 60.7 %copy-start = (bf16[1536,512]{1,0:T(8,128)(2,1)S(1)}, bf16[1536,512]{1,0:T(8,128)(2,1)}, u32[]{:S(2)}) copy-start(bf16[1536,512]{1,0:T(8,128)(2,1)} %param.15) | copy-start | bytes 4718596
  6.5 62.1 %all-gather.2.cloned.1.call-start = ((), (), s32[]{:S(2)}) async-start(), calls=%async_computation.1 | async-start | bytes 1392640 | tf_op jit(solution)/shard_map/all_gather | solution.py:39
  7.3 132.8 %reduce-scatter.2.cloned.1.call-start = ((), (), s32[]{:S(2)}) async-start(), calls=%async_computation.2 | async-start | bytes 1032192 | tf_op jit(solution)/shard_map/reduce_scatter | solution.py:102
  67.1 1.0 copy-start.1
Sparse Core Ops, SparseCore 0:
  9.6 41.9 all-gather.1
  79.8 60.2 reduce-scatter.1
where the time goes:
time: 147 us
  waiting for transfers between devices  61.1 us (42%)
  blocking collectives  54.6 us (37%)
  between operations  14.2 us (10%)
  matrix products  11.5 us (8%)
  other arithmetic  2.98 us (2%)
  local copies, waits for them, and re-layouts  2.47 us (2%)
    reduce_scatter x1, waiting for transfers between devices, shards(): lax.psum_scatter(jnp.dot(values, w_out, preferred_element_type=jnp.float3...  60.4 us
    all_gather x1, blocking collectives, shards(): q_rows = lax.all_gather(q_compressed, 'heads', axis=0, tiled=True)  32.8 us
    all_gather x1, blocking collectives, collect(): lax.all_gather(new_part, ('heads', 'query'), axis=0, tiled=True)  21.8 us
    dot_general x1, matrix products, shards(): jnp.dot(values, w_out, preferred_element_type=jnp.float32)  5.39 us
  transfers between devices with their start and end apart: 2, of which 1 were waited for; matrix products, arithmetic and copies ran while one was open for 4% of the time, Pallas kernels for 0%

commit v1 on v0

v1 whole, which is shorter than its diff:
```python
import functools

import jax
import jax.numpy as jnp
from jax import lax
from jax.experimental import pallas as pl
from jax.experimental.pallas import tpu as pltpu
from jax.sharding import PartitionSpec as P

KR = 512
RD = 64
ND = 128
VD = 128
CHUNKS = 4
LAG = 2
BF = jnp.bfloat16
F32 = jnp.float32
MESH = pl.DeviceIdType.MESH
NT = (((1,), (1,)), ((), ()))


def ring_place(h, n):
    if n != 8:
        return h
    odd = h % 2
    return (1 - odd) * (h // 2) + odd * (n - 1 - h // 2)


def ring_index(p, n):
    if n != 8:
        return p
    far = p // (n // 2)
    return (1 - far) * (2 * p) + far * (2 * (n - 1 - p) + 1)


def frequencies(shape):
    lane = lax.broadcasted_iota(jnp.int32, shape, 1) % 32
    freq = jnp.ones(shape, F32)
    for bit in range(5):
        factor = 10000.0 ** (-(2.0**bit) / 32.0)
        freq = jnp.where((lane // (2**bit)) % 2 == 1, freq * factor, freq)
    return freq


def dot(a, b):
    return jnp.dot(a, b, preferred_element_type=F32)


def kernel(
    n,
    length_ref,
    gain_ref,
    q_ref,
    new_ref,
    cache_ref,
    wqn_ref,
    wqr_ref,
    wuk_ref,
    wuv_ref,
    wo_ref,
    out_ref,
    q_all,
    new_own,
    kc,
    kf,
    wqn,
    wqr,
    wuk,
    wuv,
    wo,
    qa,
    scores,
    weights,
    o_lat,
    values,
    part,
    rs,
    load_sem,
    own_sem,
    wo_sem,
    q_send,
    q_recv,
    kc_send,
    kc_recv,
    kcs_send,
    kf_send,
    kf_recv,
    kfs_send,
    rs_send,
    rs_recv,
):
    half = n // 2
    core = lax.axis_index("query")
    other = 1 - core
    me = ring_place(lax.axis_index("heads"), n)
    right = {"heads": ring_index((me + 1) % n, n)}
    left = {"heads": ring_index((me + n - 1) % n, n)}
    sibling = {"query": other}
    way = (right, left)
    tok = q_ref.shape[0]
    slots = cache_ref.shape[0]
    piece = slots // 2
    rows = n * tok
    heads = wqn_ref.shape[1] // ND
    ctx = n * 2 * slots
    width = wo.shape[2]

    def source(direction, step):
        return (me + n - step) % n if direction == 0 else (me + step) % n

    own_q = pltpu.make_async_copy(q_ref, q_all.at[me], own_sem.at[0])
    own_new = pltpu.make_async_copy(new_ref, new_own, own_sem.at[1])
    own_cache = [
        pltpu.make_async_copy(
            cache_ref.at[pl.ds(i * piece, piece)], kc.at[me, core, i], own_sem.at[2 + i]
        )
        for i in range(2)
    ]
    own_new.start()
    own_q.start()
    for copy in own_cache:
        copy.start()
    loads = [
        pltpu.make_async_copy(src, dst, load_sem.at[i])
        for i, (src, dst) in enumerate(
            ((wqn_ref, wqn), (wqr_ref, wqr), (wuk_ref, wuk), (wuv_ref, wuv))
        )
    ]
    loads += [
        pltpu.make_async_copy(wo_ref.at[:, pl.ds(i * width, width)], wo.at[i], wo_sem.at[i])
        for i in range(CHUNKS)
    ]
    for copy in loads:
        copy.start()

    barrier = pltpu.get_barrier_semaphore()
    for target in (right, left, sibling):
        pl.semaphore_signal(barrier, inc=1, device_id=target, device_id_type=MESH)

    length = length_ref[0]
    mine = (ring_index(me, n) * 2 + core) * tok
    own_new.wait()
    latent = new_own[:, :KR].astype(F32)
    mean = jnp.mean(latent * latent, axis=-1, keepdims=True)
    latent = latent * lax.rsqrt(mean + 1e-06) * gain_ref[...][None, :]
    turned = new_own[:, KR:].astype(F32)
    position = (length + mine + lax.broadcasted_iota(jnp.int32, (tok, RD), 0)).astype(F32)
    angle = position * frequencies((tok, RD))
    swapped = jnp.concatenate([-turned[:, RD // 2 :], turned[:, : RD // 2]], axis=1)
    turned = turned * jnp.cos(angle) + swapped * jnp.sin(angle)
    kf[me, core, :, :KR] = latent.astype(BF)
    kf[me, core, :, KR:] = turned.astype(BF)

    pl.semaphore_wait(barrier, 3)

    def remote(src, dst, send, recv, target):
        return pltpu.make_async_remote_copy(
            src_ref=src, dst_ref=dst, send_sem=send, recv_sem=recv, device_id=target, device_id_type=MESH
        )

    def q_copy(direction, step, chunk):
        src = q_ref if step == 0 else q_all.at[chunk]
        return remote(
            src, q_all.at[chunk], q_send.at[direction, step], q_recv.at[chunk], way[direction]
        )

    def kc_copy(direction, step, chunk, i):
        src = cache_ref.at[pl.ds(i * piece, piece)] if step == 0 else kc.at[chunk, core, i]
        return remote(
            src,
            kc.at[chunk, core, i],
            kc_send.at[direction, step, i],
            kc_recv.at[core, chunk, i],
            way[direction],
        )

    def kf_copy(direction, step, chunk):
        return remote(
            kf.at[chunk, core],
            kf.at[chunk, core],
            kf_send.at[direction, step],
            kf_recv.at[core, chunk],
            way[direction],
        )

    def kc_across(chunk, i, owner, own=False):
        src = cache_ref.at[pl.ds(i * piece, piece)] if own else kc.at[chunk, owner, i]
        return remote(
            src, kc.at[chunk, owner, i], kcs_send.at[chunk, i], kc_recv.at[owner, chunk, i], sibling
        )

    def kf_across(chunk, owner):
        return remote(
            kf.at[chunk, owner],
            kf.at[chunk, owner],
            kfs_send.at[chunk],
            kf_recv.at[owner, chunk],
            sibling,
        )

    q_hops = (half, half - 1)
    f_hops = (half - 1, half)

    def c_hops(direction, i):
        return half if direction == i else half - 1

    sent = []

    def start(copy):
        copy.start()
        sent.append(copy)

    for d in range(2):
        start(q_copy(d, 0, me))
    for d in range(2):
        start(kf_copy(d, 0, me))
    for i in range(2):
        for d in range(2):
            start(kc_copy(d, 0, me, i))
    start(kf_across(me, core))
    for i in range(2):
        start(kc_across(me, i, core, True))

    def q_step(step):
        for d in range(2):
            if step <= q_hops[d]:
                chunk = source(d, step)
                q_copy(d, step - 1, chunk).wait_recv()
                if step < q_hops[d]:
                    start(q_copy(d, step, chunk))

    def k_step(step):
        for d in range(2):
            chunk = source(d, step)
            if step <= f_hops[d]:
                kf_copy(d, step - 1, chunk).wait_recv()
                if step < f_hops[d]:
                    start(kf_copy(d, step, chunk))
                start(kf_across(chunk, core))
        for i in range(2):
            for d in range(2):
                chunk = source(d, step)
                if step <= c_hops(d, i):
                    kc_copy(d, step - 1, chunk, i).wait_recv()
                    if step < c_hops(d, i):
                        start(kc_copy(d, step, chunk, i))
                    start(kc_across(chunk, i, core))

    for step in range(1, half + 1):
        q_step(step)
        if step > LAG:
            k_step(step - LAG)

    own_q.wait()
    loads[0].wait()
    loads[1].wait()
    q_rows = q_all[...].astype(F32).reshape(rows, q_ref.shape[1]).astype(BF)
    row = lax.broadcasted_iota(jnp.int32, (rows, 1), 0)
    row_token = (ring_index(row // tok, n) * 2 + core) * tok + row % tok
    q_nope = dot(q_rows, wqn[...]).astype(BF)
    rope = dot(q_rows, wqr[...])
    angle = (length + row_token).astype(F32) * frequencies((1, 2 * RD))
    cos = jnp.concatenate([jnp.cos(angle)] * (heads // 2), axis=1)
    sin = jnp.concatenate([jnp.sin(angle)] * (heads // 2), axis=1)
    total = heads * RD
    lane = lax.broadcasted_iota(jnp.int32, (rows, total), 1) % RD
    swapped = jnp.where(
        lane < RD // 2,
        -pltpu.roll(rope, total - RD // 2, 1),
        pltpu.roll(rope, RD // 2, 1),
    )
    rope = (rope * cos + swapped * sin).astype(BF)
    loads[2].wait()
    for h in range(heads):
        span = pl.ds(h * rows, rows)
        wk = wuk[:, h * ND : (h + 1) * ND]
        qa[span, :KR] = lax.dot_general(
            q_nope[:, h * ND : (h + 1) * ND], wk, NT, preferred_element_type=F32
        ).astype(BF)
        qa[span, KR:] = rope[:, h * RD : (h + 1) * RD]

    scale = (ND + RD) ** (-0.5)

    def score(chunk):
        keys = kc[chunk].reshape(2 * slots, KR + RD)
        value = lax.dot_general(qa[...], keys, NT, preferred_element_type=F32) * scale
        kidx = ring_index(chunk, n) * (2 * slots) + lax.broadcasted_iota(
            jnp.int32, (1, 2 * slots), 1
        )
        at = pl.multiple_of(chunk * (2 * slots), 2 * slots)
        scores[:, pl.ds(at, 2 * slots)] = jnp.where(kidx < length, value, -1e30)

    def sibling_step(chunk):
        kf_across(chunk, other).wait_recv()
        for i in range(2):
            kc_across(chunk, i, other).wait_recv()

    for copy in own_cache:
        copy.wait()
    sibling_step(me)
    if n == 8:
        score(me)
    for step in range(1, half + 1):
        if step > half - LAG:
            k_step(step)
        for d in range(2):
            if d == 0 or step < half:
                sibling_step(source(d, step))
                if n == 8:
                    score(source(d, step))
    if n != 8:
        lax.fori_loop(0, n, lambda p, carry: (score(p), carry)[1], 0)

    fresh = kf[...].astype(F32).reshape(2 * rows, KR + RD).astype(BF)
    value = lax.dot_general(qa[...], fresh, NT, preferred_element_type=F32) * scale
    key = lax.broadcasted_iota(jnp.int32, (1, 2 * rows), 1)
    key_token = ring_index(key // (2 * tok), n) * (2 * tok) + key % (2 * tok)
    row = lax.broadcasted_iota(jnp.int32, (heads * rows, 1), 0) % rows
    row_token = (ring_index(row // tok, n) * 2 + core) * tok + row % tok
    scores[:, pl.ds(ctx, 2 * rows)] = jnp.where(key_token <= row_token, value, -1e30)

    block = weights.shape[0]
    strip = 64

    def attend(b, carry):
        base = b * block

        def soften(r, inner):
            s = scores[pl.ds(pl.multiple_of(base + r * strip, strip), strip), :]
            e = jnp.exp(s - jnp.max(s, axis=-1, keepdims=True))
            e = e * (1.0 / jnp.sum(e, axis=-1, keepdims=True))
            weights[pl.ds(pl.multiple_of(r * strip, strip), strip), :] = e.astype(BF)
            return inner

        lax.fori_loop(0, block // strip, soften, 0)
        latents = kc[:, :, :, :, :KR].reshape(ctx, KR)
        o = dot(weights[:, :ctx], latents) + dot(weights[:, ctx:], fresh[:, :KR])
        o_lat[pl.ds(pl.multiple_of(base, block), block), :] = o.astype(BF)
        return carry

    lax.fori_loop(0, heads * rows // block, attend, 0)

    loads[3].wait()
    for h in range(heads):
        values[:, h * VD : (h + 1) * VD] = dot(
            o_lat[pl.ds(h * rows, rows), :], wuv[:, h * VD : (h + 1) * VD]
        ).astype(BF)

    def sum_hops(d, c):
        return half if (d == 0) == (c < CHUNKS // 2) else half - 1

    def toward(d, distance):
        return (me + distance) % n if d == 0 else (me + n - distance) % n

    def rs_copy(d, t, c):
        src = part.at[toward(d, sum_hops(d, c)), c] if t == 0 else rs.at[d, t - 1, c]
        return remote(src, rs.at[d, t, c], rs_send.at[d, t, c], rs_recv.at[d, t, c], way[d])

    for c in range(CHUNKS):
        loads[4 + c].wait()
        value = dot(values[...], wo[c])
        part[:, c] = value.reshape(n, tok, width).astype(BF)
        for d in range(2):
            start(rs_copy(d, 0, c))
    for t in range(1, half + 1):
        for c in range(CHUNKS):
            for d in range(2):
                hops = sum_hops(d, c)
                if t < hops:
                    rs_copy(d, t - 1, c).wait_recv()
                    held = rs[d, t - 1, c].astype(F32) + part[toward(d, hops - t), c].astype(F32)
                    rs[d, t - 1, c] = held.astype(BF)
                    start(rs_copy(d, t, c))
    for c in range(CHUNKS):
        total_value = part[me, c].astype(F32)
        for d in range(2):
            hops = sum_hops(d, c)
            rs_copy(d, hops - 1, c).wait_recv()
            total_value = total_value + rs[d, hops - 1, c].astype(F32)
        out_ref[:, c * width : (c + 1) * width] = total_value.astype(BF)
    for copy in sent:
        copy.wait_send()


def shards(
    n,
    q_compressed,
    new_latent,
    cached_latent,
    latent_gain,
    cached_length,
    w_q_nope,
    w_q_rope,
    w_uk,
    w_uv,
    w_out,
):
    tok, qr = q_compressed.shape
    slots, kw = cached_latent.shape
    heads = w_q_nope.shape[1] // ND
    depth, model = w_out.shape
    rows = n * tok
    ctx = n * 2 * slots
    half = n // 2
    width = model // CHUNKS
    hbm = pl.BlockSpec(memory_space=pl.ANY)
    vmem = pl.BlockSpec(memory_space=pltpu.VMEM)
    dma = pltpu.SemaphoreType.DMA
    block = min(256, heads * rows)
    return pl.pallas_call(
        functools.partial(kernel, n),
        out_shape=jax.ShapeDtypeStruct((tok, model), BF),
        in_specs=[pl.BlockSpec(memory_space=pltpu.SMEM), vmem] + [hbm] * 8,
        out_specs=vmem,
        scratch_shapes=[
            pltpu.VMEM((n, tok, qr), BF),
            pltpu.VMEM((tok, kw), BF),
            pltpu.VMEM((n, 2, 2, slots // 2, kw), BF),
            pltpu.VMEM((n, 2, tok, kw), BF),
            pltpu.VMEM(w_q_nope.shape, BF),
            pltpu.VMEM(w_q_rope.shape, BF),
            pltpu.VMEM(w_uk.shape, BF),
            pltpu.VMEM(w_uv.shape, BF),
            pltpu.VMEM((CHUNKS, depth, width), BF),
            pltpu.VMEM((heads * rows, kw), BF),
            pltpu.VMEM((heads * rows, ctx + 2 * rows), F32),
            pltpu.VMEM((block, ctx + 2 * rows), BF),
            pltpu.VMEM((heads * rows, KR), BF),
            pltpu.VMEM((rows, heads * VD), BF),
            pltpu.VMEM((n, CHUNKS, tok, width), BF),
            pltpu.VMEM((2, half, CHUNKS, tok, width), BF),
            dma((4,)),
            dma((4,)),
            dma((CHUNKS,)),
            dma((2, half)),
            dma((n,)),
            dma((2, half, 2)),
            dma((2, n, 2)),
            dma((n, 2)),
            dma((2, half)),
            dma((2, n)),
            dma((n,)),
            dma((2, half, CHUNKS)),
            dma((2, half, CHUNKS)),
        ],
        compiler_params=pltpu.CompilerParams(
            collective_id=0, has_side_effects=True, vmem_limit_bytes=60 * 1024 * 1024
        ),
    )(
        cached_length,
        latent_gain,
        q_compressed,
        new_latent,
        cached_latent,
        w_q_nope,
        w_q_rope,
        w_uk,
        w_uv,
        w_out,
    )


def solution(mesh):
    placed = (
        P(("groups", "heads", "query"), None),
        P(("groups", "heads", "query"), None),
        P(("groups", "heads", "query"), None),
        P(),
        P("groups"),
        P(None, "heads"),
        P(None, "heads"),
        P(None, "heads"),
        P(None, "heads"),
        P("heads", None),
    )
    return jax.shard_map(
        functools.partial(shards, mesh.shape["heads"]),
        mesh=mesh,
        in_specs=placed,
        out_specs=P(("groups", "heads", "query"), None),
        check_vma=False,
    )
```

time: 147 us -> 45.8 us (0.31)
  waiting for transfers between devices: 61.1 us -> 0 us
  blocking collectives: 54.6 us -> 0 us
  Pallas kernels: 0 us -> 43.4 us
  between operations: 14.2 us -> 0.66 us
  matrix products: 11.5 us -> 0 us
  other arithmetic: 2.98 us -> 0 us
    reduce_scatter x1 -> x0, waiting for transfers between devices: 60.4 us -> none  [shards(): lax.psum_scatter(jnp.dot(values, w_out, preferred_element_type=jnp.float3...]
    all_gather x2 -> x0, blocking collectives: 54.6 us -> none  [the longest x1 32.8 us: shards(): q_rows = lax.all_gather(q_compressed, 'heads', axis=0, tiled=True)]
    pallas_call x0 -> x1, Pallas kernels: none -> 43.4 us  [shards(): pl.pallas_call(functools.partial(kernel, n), out_shape=jax.ShapeDtypeStru...]
    dot_general x5 -> x0, matrix products: 9.57 us -> none  [the longest x1 5.39 us: shards(): jnp.dot(values, w_out, preferred_element_type=jnp.float32)]
    sub x1 -> x0, matrix products: 1.93 us -> none  [shards(): expo = jnp.exp(scores - top)]
    all_gather x2 -> x0, local copies, waits for them, and re-layouts: 1.72 us -> none  [the longest x1 1.57 us: collect(): lax.all_gather(cached_part, ('heads', 'query'), axis=0, tiled=True)]
  transfers between devices with their start and end apart: 2 -> 0, of which waited for: 1 -> 0; matrix products, arithmetic and copies ran while one was open for 4% -> 0% of each run, Pallas kernels for 0% -> 0%
where the time goes in v1:
time: 45.8 us; the launch traced here: 45.6 us
  Pallas kernels  43.4 us (95%)
  local copies, waits for them, and re-layouts  1.55 us (3%)
  between operations  0.66 us (1%)
    pallas_call x1, Pallas kernels, shards(): pl.pallas_call(functools.partial(kernel, n), out_shape=jax.ShapeDtypeStru...  43.4 us
    unnamed x1, local copies, waits for them, and re-layouts  1.55 us

profile of v1, /device:TPU:0, one launch (start us, length us, event | category | flops | bytes accessed | tf_op | source)
XLA Modules:
  0.0 45.6 jit_solution(11465239673460007608)
XLA Ops:
  0.7 43.4 %shard_map.100 = bf16[8,7168]{1,0:T(8,128)(2,1)} custom-call(s32[1]{0:T(128)S(6)} %copy.12.length_ref, f32[512]{0:T(512)} %gain_ref.1, bf16[8,1536]{1,0:T(8,128)(2,1)} %q_ref.1, bf16[8,576]{1,0:T(8,128)(2,1)} %new_ref.1, bf16[64,576]{1,0:T(8,128)(2,1)} %cache_ref.1, bf16[1536,512]{1,0:T(8,128)(2,1)} %wqn_ref.1, bf16[1536,256]{1,0:T(8,128)(2,1)} %wqr_ref.1, ...), custom_call_target="tpu_custom_call" | custom-call | tf_op jit(solution)/shard_map/pallas_call | solution.py:410
  44.0 1.6 %copy.13 = bf16[8,7168]{1,0:T(8,128)(2,1)} copy(bf16[8,7168]{1,0:T(8,128)(2,1)} %shard_map.100) | data formatting | bytes 229376

commit v2 on v1

--- a/solution.py
+++ b/solution.py
@@ -12,7 +12,7 @@
 ND = 128
 VD = 128
 CHUNKS = 4
-LAG = 2
+LAG = 1
 BF = jnp.bfloat16
 F32 = jnp.float32
 MESH = pl.DeviceIdType.MESH
@@ -130,8 +130,6 @@
         pltpu.make_async_copy(wo_ref.at[:, pl.ds(i * width, width)], wo.at[i], wo_sem.at[i])
         for i in range(CHUNKS)
     ]
-    for copy in loads:
-        copy.start()
 
     barrier = pltpu.get_barrier_semaphore()
     for target in (right, left, sibling):
@@ -220,6 +218,9 @@
     start(kf_across(me, core))
     for i in range(2):
         start(kc_across(me, i, core, True))
+
+    for copy in loads:
+        copy.start()
 
     def q_step(step):
         for d in range(2):
@@ -248,7 +249,7 @@
 
     for step in range(1, half + 1):
         q_step(step)
-        if step > LAG:
+        if LAG < step < half:
             k_step(step - LAG)
 
     own_q.wait()
@@ -259,6 +260,7 @@
     row_token = (ring_index(row // tok, n) * 2 + core) * tok + row % tok
     q_nope = dot(q_rows, wqn[...]).astype(BF)
     rope = dot(q_rows, wqr[...])
+    k_step(half - 1)
     angle = (length + row_token).astype(F32) * frequencies((1, 2 * RD))
     cos = jnp.concatenate([jnp.cos(angle)] * (heads // 2), axis=1)
     sin = jnp.concatenate([jnp.sin(angle)] * (heads // 2), axis=1)

time: 45.8 us -> 43.7 us (0.954)
  Pallas kernels: 43.4 us -> 41.3 us
    pallas_call x1, Pallas kernels: 43.4 us -> 41.3 us  [shards(): pl.pallas_call(functools.partial(kernel, n), out_shape=jax.ShapeDtypeStru...]
where the time goes in v2:
time: 43.7 us; the launch traced here: 43.5 us
  Pallas kernels  41.3 us (95%)
  local copies, waits for them, and re-layouts  1.55 us (4%)
  between operations  0.66 us (2%)
    pallas_call x1, Pallas kernels, shards(): pl.pallas_call(functools.partial(kernel, n), out_shape=jax.ShapeDtypeStru...  41.3 us
    unnamed x1, local copies, waits for them, and re-layouts  1.55 us

profile of v2, /device:TPU:0, one launch (start us, length us, event | category | flops | bytes accessed | tf_op | source)
XLA Modules:
  0.0 43.5 jit_solution(2268125360474880915)
XLA Ops:
  0.7 41.3 %shard_map.100 = bf16[8,7168]{1,0:T(8,128)(2,1)} custom-call(s32[1]{0:T(128)S(6)} %copy.12.length_ref, f32[512]{0:T(512)} %gain_ref.1, bf16[8,1536]{1,0:T(8,128)(2,1)} %q_ref.1, bf16[8,576]{1,0:T(8,128)(2,1)} %new_ref.1, bf16[64,576]{1,0:T(8,128)(2,1)} %cache_ref.1, bf16[1536,512]{1,0:T(8,128)(2,1)} %wqn_ref.1, bf16[1536,256]{1,0:T(8,128)(2,1)} %wqr_ref.1, ...), custom_call_target="tpu_custom_call" | custom-call | tf_op jit(solution)/shard_map/pallas_call | solution.py:412
  41.9 1.6 %copy.13 = bf16[8,7168]{1,0:T(8,128)(2,1)} copy(bf16[8,7168]{1,0:T(8,128)(2,1)} %shard_map.100) | data formatting | bytes 229376

commit v3 on v2

--- a/solution.py
+++ b/solution.py
@@ -11,7 +11,8 @@
 RD = 64
 ND = 128
 VD = 128
-CHUNKS = 4
+CHUNKS = 8
+BEHIND = 5
 LAG = 1
 BF = jnp.bfloat16
 F32 = jnp.float32
@@ -358,21 +359,26 @@
         src = part.at[toward(d, sum_hops(d, c)), c] if t == 0 else rs.at[d, t - 1, c]
         return remote(src, rs.at[d, t, c], rs_send.at[d, t, c], rs_recv.at[d, t, c], way[d])
 
+    def pass_on(t, c):
+        for d in range(2):
+            hops = sum_hops(d, c)
+            if t < hops:
+                rs_copy(d, t - 1, c).wait_recv()
+                held = rs[d, t - 1, c].astype(F32) + part[toward(d, hops - t), c].astype(F32)
+                rs[d, t - 1, c] = held.astype(BF)
+                start(rs_copy(d, t, c))
+
     for c in range(CHUNKS):
         loads[4 + c].wait()
         value = dot(values[...], wo[c])
         part[:, c] = value.reshape(n, tok, width).astype(BF)
         for d in range(2):
             start(rs_copy(d, 0, c))
+        if c >= BEHIND:
+            pass_on(1, c - BEHIND)
     for t in range(1, half + 1):
-        for c in range(CHUNKS):
-            for d in range(2):
-                hops = sum_hops(d, c)
-                if t < hops:
-                    rs_copy(d, t - 1, c).wait_recv()
-                    held = rs[d, t - 1, c].astype(F32) + part[toward(d, hops - t), c].astype(F32)
-                    rs[d, t - 1, c] = held.astype(BF)
-                    start(rs_copy(d, t, c))
+        for c in range(CHUNKS - BEHIND if t == 1 else 0, CHUNKS):
+            pass_on(t, c)
     for c in range(CHUNKS):
         total_value = part[me, c].astype(F32)
         for d in range(2):

time: 43.7 us -> 45.1 us (1.032)
  Pallas kernels: 41.3 us -> 42.6 us
    pallas_call x1, Pallas kernels: 41.3 us -> 42.6 us  [shards(): pl.pallas_call(functools.partial(kernel, n), out_shape=jax.ShapeDtypeStru...]
where the time goes in v3:
time: 45.1 us; the launch traced here: 44.8 us
  Pallas kernels  42.6 us (94%)
  local copies, waits for them, and re-layouts  1.55 us (3%)
  between operations  0.66 us (1%)
    pallas_call x1, Pallas kernels, shards(): pl.pallas_call(functools.partial(kernel, n), out_shape=jax.ShapeDtypeStru...  42.6 us
    unnamed x1, local copies, waits for them, and re-layouts  1.55 us

profile of v3, /device:TPU:0, one launch (start us, length us, event | category | flops | bytes accessed | tf_op | source)
XLA Modules:
  0.0 44.8 jit_solution(12590122156297054409)
XLA Ops:
  0.7 42.6 %shard_map.100 = bf16[8,7168]{1,0:T(8,128)(2,1)} custom-call(s32[1]{0:T(128)S(6)} %copy.12.length_ref, f32[512]{0:T(512)} %gain_ref.1, bf16[8,1536]{1,0:T(8,128)(2,1)} %q_ref.1, bf16[8,576]{1,0:T(8,128)(2,1)} %new_ref.1, bf16[64,576]{1,0:T(8,128)(2,1)} %cache_ref.1, bf16[1536,512]{1,0:T(8,128)(2,1)} %wqn_ref.1, bf16[1536,256]{1,0:T(8,128)(2,1)} %wqr_ref.1, ...), custom_call_target="tpu_custom_call" | custom-call | tf_op jit(solution)/shard_map/pallas_call | solution.py:418
  43.3 1.6 %copy.13 = bf16[8,7168]{1,0:T(8,128)(2,1)} copy(bf16[8,7168]{1,0:T(8,128)(2,1)} %shard_map.100) | data formatting | bytes 229376
